TPU v7x, 256 devices: a whole 4x4x8 slice. The times are simulated.
256 devices in a mesh: sx: 4 (over x_lo, core), sy: 2 (over x_hi), fsdp: 32 (over z, y).
Axes of the slice: x: 4 (x_hi: 2, x_lo: 2; x = x_hi * 2 + x_lo), y: 4, z: 8, core: 2. Of those that a mesh axis runs over, the one named last changes fastest.
Arguments:
- x_code: bfloat16 [32, 32, 32, 1536], P('fsdp', 'sx', 'sy'), may hold values from -6 to 6
- x_exp: int32 [32, 32, 32, 12], P('fsdp', 'sx', 'sy'), may hold values from -2 to 2
- dw_kernel: float32 [7, 7, 1536], replicated, may hold values from -1.2 to 1.2
- dw_bias: float32 [1536], replicated, may hold values from -4 to 4
- ln_gain: float32 [1536], replicated, may hold values from 0.1 to 1.9
- ln_bias: float32 [1536], replicated, may hold values from -3 to 3
- w_up: bfloat16 [1536, 3072], P('fsdp'), may hold values from -0.15625 to 0.15625
- b_up: float32 [3072], replicated, may hold values from -3 to 3
- w_down: bfloat16 [3072, 1536], P(None, 'fsdp'), may hold values from -0.109375 to 0.109375
- b_down: float32 [1536], replicated, may hold values from -3 to 3
- layer_scale: float32 [1536], replicated, may hold values from 0.3 to 1.5
- cotangent: bfloat16 [32, 32, 32, 1536], P('fsdp', 'sx', 'sy'), may hold values from -6 to 6
Outputs:
- block_out: bfloat16 [32, 32, 32, 1536], P('fsdp', 'sx', 'sy')
- grad_input: bfloat16 [32, 32, 32, 1536], P('fsdp', 'sx', 'sy')
- grad_kernel: float32 [7, 7, 1536], replicated
- grad_gain: float32 [1536], replicated
- grad_scale: float32 [1536], replicated
All inputs are finite; a program needn't handle non-finite values.
Results may differ from a plain program's by a relative error of at most 0.006.
Values may be sent and summed in bfloat16 or wider, within the bound.
A program may use at most 192 MiB of HBM per device.

v0:
```python
import jax
import jax.numpy as jnp
from jax import lax
from jax.sharding import PartitionSpec as P

CG = 128
KW = 7


def with_halo(shard, sides, width):
    for axis, dim in sides:
        devices, length = (lax.axis_size(axis), shard.shape[dim])
        up = [(i, (i + 1) % devices) for i in range(devices - 1)]
        down = [(j, i) for i, j in up]
        last = lax.slice_in_dim(shard, length - width, length, axis=dim)
        initial = lax.slice_in_dim(shard, 0, width, axis=dim)
        before = lax.ppermute(last, axis, up)
        after = lax.ppermute(initial, axis, down)
        shard = jnp.concatenate([before, shard, after], axis=dim)
    return shard


def gelu_tanh(v):
    return jax.nn.gelu(v, approximate=True)


def on_device(
    x_code,
    x_exp,
    dw_kernel,
    dw_bias,
    ln_gain,
    ln_bias,
    w_up,
    b_up,
    w_down,
    b_down,
    layer_scale,
    cotangent,
):
    code = x_code[0]
    rows, cols, chans = code.shape
    factor = jnp.exp2(x_exp[0].astype(jnp.float32))
    grouped = code.astype(jnp.float32).reshape(rows, cols, chans // CG, CG) * factor[..., None]
    scaled = grouped.reshape(rows, cols, chans).astype(jnp.bfloat16)
    up_full, down_full = (
        lax.all_gather(w_up, "fsdp", axis=0, tiled=True),
        lax.all_gather(w_down, "fsdp", axis=1, tiled=True),
    )
    padded_x = with_halo(scaled[None], (("sx", 1), ("sy", 2)), 3)[0].astype(jnp.float32)
    conv = jnp.zeros((rows, cols, chans), jnp.float32) + dw_bias
    for i in range(KW):
        for j in range(KW):
            conv = conv + dw_kernel[i, j] * padded_x[i : i + rows, j : j + cols]
    mean_val = jnp.mean(conv, axis=-1, keepdims=True)
    centred = conv - mean_val
    rstd = lax.rsqrt(jnp.mean(centred * centred, axis=-1, keepdims=True) + 1e-06)
    normed = centred * rstd
    ln_out = (normed * ln_gain + ln_bias).astype(jnp.bfloat16).reshape(rows * cols, chans)
    pre = jnp.dot(ln_out, up_full, preferred_element_type=jnp.float32) + b_up
    act, gelu_back = jax.vjp(gelu_tanh, pre)
    mlp = jnp.dot(act.astype(jnp.bfloat16), down_full, preferred_element_type=jnp.float32) + b_down
    mlp = mlp.reshape(rows, cols, chans)
    block_out = (scaled.astype(jnp.float32) + layer_scale * mlp).astype(jnp.bfloat16)
    grad_f = cotangent[0].astype(jnp.float32)
    scale_term = jnp.sum(grad_f * mlp, axis=(0, 1))
    d_mlp = (layer_scale * grad_f).astype(jnp.bfloat16).reshape(rows * cols, chans)
    d_act = lax.dot_general(
        d_mlp, down_full, (((1,), (1,)), ((), ())), preferred_element_type=jnp.float32
    )
    d_pre = gelu_back(d_act)[0].astype(jnp.bfloat16)
    d_ln = lax.dot_general(
        d_pre, up_full, (((1,), (1,)), ((), ())), preferred_element_type=jnp.float32
    )
    d_ln = d_ln.reshape(rows, cols, chans)
    gain_term = jnp.sum(d_ln * normed, axis=(0, 1))
    d_norm = d_ln * ln_gain
    d_conv = rstd * (
        d_norm
        - jnp.mean(d_norm, axis=-1, keepdims=True)
        - normed * jnp.mean(d_norm * normed, axis=-1, keepdims=True)
    )
    kernel_rows = []
    for i in range(KW):
        kernel_cols = []
        for j in range(KW):
            kernel_cols.append(jnp.sum(d_conv * padded_x[i : i + rows, j : j + cols], axis=(0, 1)))
        kernel_rows.append(jnp.stack(kernel_cols))
    kernel_term = jnp.stack(kernel_rows)
    padded_grad = with_halo(d_conv[None].astype(jnp.bfloat16), (("sx", 1), ("sy", 2)), 3).astype(
        jnp.float32
    )[0]
    back_conv = grad_f
    for i in range(KW):
        for j in range(KW):
            back_conv = (
                back_conv
                + dw_kernel[i, j] * padded_grad[6 - i : 6 - i + rows, 6 - j : 6 - j + cols]
            )
    grad_input = back_conv.astype(jnp.bfloat16)
    grad_kernel, grad_gain, grad_scale = lax.psum(
        (kernel_term, gain_term, scale_term), ("sx", "sy", "fsdp")
    )
    return (block_out[None], grad_input[None], grad_kernel, grad_gain, grad_scale)


def solution(mesh):
    placed = (
        P("fsdp", "sx", "sy", None),
        P("fsdp", "sx", "sy", None),
        P(),
        P(),
        P(),
        P(),
        P("fsdp", None),
        P(),
        P(None, "fsdp"),
        P(),
        P(),
        P("fsdp", "sx", "sy", None),
    )
    return jax.shard_map(
        on_device,
        mesh=mesh,
        in_specs=placed,
        out_specs=(P("fsdp", "sx", "sy", None), P("fsdp", "sx", "sy", None), P(), P(), P()),
        check_vma=False,
    )
```

profile of v0, /device:TPU:1, one launch (start us, length us, event | category | flops | bytes accessed | tf_op | source)
XLA Modules:
  0.0 522.2 jit_solution(14191568544540321584)
XLA Ops:
  7.2 0.7 all-gather.3.cloned.1.call-update
  7.9 0.7 all-gather.5.cloned.1.call-update
  8.7 0.9 exponential_bitcast_fusion
  9.6 0.1 copy.18
  9.7 0.3 mul.1066
  10.0 0.1 mul.1067
  10.3 4.5 collective-permute-start
  14.8 1.9 collective-permute-start.1
  16.8 0.3 slice_reduce_fusion.48
  17.2 0.9 slice_reduce_fusion.47
  18.3 3.0 collective-permute-done.1
  21.3 0.1 pad_maximum_fusion.3
  21.4 4.4 collective-permute-start.2
  25.8 1.3 collective-permute-start.3
  27.1 0.8 slice_reduce_fusion.46
  27.8 0.2 collective-permute-done.2
  28.1 5.4 %collective-permute-done.3 = bf16[1,14,3,1536]{3,2,1,0:T(4,128)(2,1)S(1)} collective-permute-done((bf16[1,14,3,1536]{3,2,1,0:T(4,128)(2,1)S(1)}, bf16[1,14,3,1536]{3,2,1,0:T(4,128)(2,1)S(1)}, u32[]{:S(2)}, u32[]{:S(2)}) %collective-permute-start.3) | collective-permute-done | bytes 129056 | tf_op jit(solution)/shard_map/ppermute | solution.py:18
  33.5 0.4 fusion.7
  34.2 9.4 %fusion.84 = (f32[8,16]{1,0:T(8,128)S(1)}, f32[8,16,1536]{2,1,0:T(8,128)S(1)}) fusion(f32[14,22,1536]{2,1,0:T(8,128)S(1)} %fusion.7, f32[1536]{0:T(1024)} %get-tuple-element.103, f32[1536]{0:T(1024)} %get-tuple-element.104, f32[1536]{0:T(1024)S(1)} %get-tuple-element.57, f32[1536]{0:T(1024)S(1)} %get-tuple-element.58, f32[1536]{0:T(1024)S(1)} %get-tuple-element.59, ...), kind=kLoop, calls=%fused_computation.267 | loop fusion | flops 19464064 | bytes 39629312 | tf_op jit(solution)/shard_map/reduce_sum | solution.py:55
  43.7 0.2 multiply_reduce_fusion.52
  43.9 1.7 add_convert_fusion.1
  45.6 71.9 %all-gather.3.cloned.1.call-done = bf16[1536,3072]{1,0:T(8,128)(2,1)} async-done(((bf16[48,3072]{1,0:T(8,128)(2,1)}), bf16[1536,3072]{1,0:T(8,128)(2,1)}) %all-gather.3.cloned.1.call-update) | async-done | bytes 9437200 | tf_op jit(solution)/shard_map/all_gather | solution.py:47
  117.5 6.4 %convolution_add_fusion = f32[128,3072]{1,0:T(8,128)} fusion(bf16[128,1536]{1,0:T(8,128)(2,1)} %bitcast.55, bf16[1536,3072]{1,0:T(8,128)(2,1)} %all-gather.3.cloned.1.call-done, f32[3072]{0:T(1024)S(1)} %copy-done.50), kind=kOutput, calls=%fused_computation | convolution fusion | flops 1208352768 | bytes 11415552 | tf_op jit(solution)/shard_map/dot_general | solution.py:60
  124.0 96.8 %all-gather.5.cloned.1.call-done = bf16[3072,1536]{0,1:T(8,128)(2,1)} async-done(((bf16[3072,48]{0,1:T(8,128)(2,1)}), bf16[3072,1536]{0,1:T(8,128)(2,1)}) %all-gather.5.cloned.1.call-update) | async-done | bytes 9437200 | tf_op jit(solution)/shard_map/all_gather | solution.py:48
  220.8 8.9 %fusion.61 = (f32[1536]{0:T(1024)}, bf16[128,1536]{1,0:T(8,128)(2,1)}, f32[128,1536]{1,0:T(8,128)}) fusion(bf16[1,8,16,1536]{3,2,1,0:T(8,128)(2,1)} %param.23, f32[1536]{0:T(1024)S(1)} %copy-done.51, f32[1536]{0:T(1024)S(1)} %copy-done.54, bf16[3072,1536]{0,1:T(8,128)(2,1)} %all-gather.5.cloned.1.call-done, f32[128,3072]{1,0:T(8,128)} %convolution_add_fusion), kind=kOutput, calls=%fused_computation.119 | convolution fusion | flops 1212676608 | bytes 12601344 | tf_op jit(solution)/shard_map/dot_general | solution.py:62
  229.7 13.3 %multiply_reduce_fusion.51 = (f32[128]{0:T(128)S(1)}, f32[128,1536]{1,0:T(8,128)}) fusion(f32[1536]{0:T(1024)S(1)} %copy-done.8, bf16[1536,3072]{1,0:T(8,128)(2,1)} %all-gather.3.cloned.1.call-done, f32[128,3072]{1,0:T(8,128)} %convolution_add_fusion, bf16[128,1536]{1,0:T(8,128)(2,1)} %get-tuple-element.118, ...), kind=kOutput, calls=%fused_computation.172 | convolution fusion | flops 2424176640 | bytes 21633536 | tf_op jit(solution)/shard_map/dot_general | solution.py:72
  243.0 0.1 div.17
  243.1 2.4 multiply_reduce_fusion
  245.5 2.6 multiply_reduce_fusion.1
  248.1 1.4 multiply_reduce_fusion.37
  249.6 2.0 multiply_reduce_fusion.19
  251.6 0.9 add_convert_fusion
  253.1 4.1 collective-permute-start.4
  257.2 1.9 collective-permute-start.5
  259.2 0.1 stack.217
  259.3 0.1 stack.226
  259.8 3.9 collective-permute-done.5
  263.7 0.1 fusion.83
  263.8 0.1 fusion.85
  263.9 4.3 collective-permute-start.6
  268.3 1.3 collective-permute-start.7
  269.6 0.7 copy-done.2
  270.4 75.8 %all-reduce = (f32[1536]{0:T(1024)}, f32[1536]{0:T(1024)}) all-reduce(f32[1536]{0:T(1024)S(1)} %copy-done.49, f32[1536]{0:T(1024)S(1)} %copy-done.53), channel_id=1, replica_groups=mesh['sx'=4,'sy'=2,'fsdp'=32] {'sx','sy','fsdp'}, use_global_device_ids=true, to_apply=%region_55.0 | all-reduce | flops 3072 | bytes 24576 | tf_op jit(solution)/shard_map/psum | solution.py:101
  346.3 0.6 copy-done.6
  347.0 1.4 maximum_convert_fusion
  348.4 7.7 %fusion.72 = bf16[1,8,16,1536]{3,2,1,0:T(8,128)(2,1)} fusion(f32[14,22,1536]{2,1,0:T(8,128)S(1)} %maximum_convert_fusion, f32[1536]{0:T(1024)} %get-tuple-element.103, f32[1536]{0:T(1024)} %get-tuple-element.104, f32[1536]{0:T(1024)S(1)} %get-tuple-element.57, f32[1536]{0:T(1024)S(1)} %copy-done.10, f32[1536]{0:T(1024)S(1)} %copy-done.12, ...), kind=kLoop, calls=%fused_computation.191 | loop fusion | flops 19660800 | bytes 39622656 | tf_op jit(solution)/shard_map/broadcast_in_dim | solution.py:104
  356.1 157.8 %all-reduce.3.cloned.1.call-done = f32[7,7,1536]{2,1,0:T(8,128)} async-done(((f32[7,7,1536]{2,1,0:T(8,128)}), f32[7,7,1536]{2,1,0:T(8,128)}) %all-reduce.3.cloned.1.call-update) | async-done | bytes 301072 | tf_op jit(solution)/shard_map/psum | solution.py:101
  514.0 1.7 copy.26
  (184 shorter events, 1.3 us)
Async XLA Ops:
  7.2 110.4 %all-gather.3.cloned.1.call-start = ((), (), s32[]{:S(2)}) async-start(), calls=%async_computation | async-start | bytes 9732096 | tf_op jit(solution)/shard_map/all_gather | solution.py:47
  7.9 212.9 %all-gather.5.cloned.1.call-start = ((), (), s32[]{:S(2)}) async-start(), calls=%async_computation.1 | async-start | bytes 9732096 | tf_op jit(solution)/shard_map/all_gather | solution.py:48
  8.7 505.3 %all-reduce.3.cloned.1.call-start = ((), (), s32[]{:S(2)}) async-start(), calls=%async_computation.2 | async-start | bytes 688128 | tf_op jit(solution)/shard_map/psum | solution.py:101
  10.3 8.0 %collective-permute-start = (bf16[1,3,16,1536]{3,2,1,0:T(8,128)(2,1)S(1)}, bf16[1,3,16,1536]{3,2,1,0:T(8,128)(2,1)S(1)}, u32[]{:S(2)}, u32[]{:S(2)}) collective-permute-start(bf16[1,3,16,1536]{3,2,1,0:T(8,128)(2,1)S(1)} %get-tuple-element.121), channel_id=1, source_target_pairs={{0,64},{64,128},{128,192},{1,65},{65,129},{129,193},{2,66},{66,130... | collective-permute-start | bytes 442376 | tf_op jit(solution)/shard_map/ppermute | solution.py:17
  14.8 6.5 %collective-permute-start.1 = (bf16[1,3,16,1536]{3,2,1,0:T(8,128)(2,1)S(1)}, bf16[1,3,16,1536]{3,2,1,0:T(8,128)(2,1)S(1)}, u32[]{:S(2)}, u32[]{:S(2)}) collective-permute-start(bf16[1,3,16,1536]{3,2,1,0:T(8,128)(2,1)S(1)} %get-tuple-element.122), channel_id=1, source_target_pairs={{64,0},{128,64},{192,128},{65,1},{129,65},{193,129},{66,2},{130,66... | collective-permute-start | bytes 442376 | tf_op jit(solution)/shard_map/ppermute | solution.py:18
  17.1 16.8 %copy-start.9 = (f32[1536]{0:T(1024)}, f32[1536]{0:T(1024)S(1)}, u32[]{:S(2)}) copy-start(f32[1536]{0:T(1024)S(1)} %get-tuple-element.58) | copy-start | bytes 18436
  17.1 16.8 %copy-start.11 = (f32[1536]{0:T(1024)}, f32[1536]{0:T(1024)S(1)}, u32[]{:S(2)}) copy-start(f32[1536]{0:T(1024)S(1)} %get-tuple-element.59) | copy-start | bytes 18436
  17.1 16.8 %copy-start.13 = (f32[1536]{0:T(1024)}, f32[1536]{0:T(1024)S(1)}, u32[]{:S(2)}) copy-start(f32[1536]{0:T(1024)S(1)} %get-tuple-element.60) | copy-start | bytes 18436
  17.1 16.8 %copy-start.15 = (f32[1536]{0:T(1024)}, f32[1536]{0:T(1024)S(1)}, u32[]{:S(2)}) copy-start(f32[1536]{0:T(1024)S(1)} %get-tuple-element.61) | copy-start | bytes 18436
  17.1 16.8 %copy-start.17 = (f32[1536]{0:T(1024)}, f32[1536]{0:T(1024)S(1)}, u32[]{:S(2)}) copy-start(f32[1536]{0:T(1024)S(1)} %get-tuple-element.62) | copy-start | bytes 18436
  17.1 16.8 %copy-start.19 = (f32[1536]{0:T(1024)}, f32[1536]{0:T(1024)S(1)}, u32[]{:S(2)}) copy-start(f32[1536]{0:T(1024)S(1)} %get-tuple-element.63) | copy-start | bytes 18436
  17.1 16.8 %copy-start.21 = (f32[1536]{0:T(1024)}, f32[1536]{0:T(1024)S(1)}, u32[]{:S(2)}) copy-start(f32[1536]{0:T(1024)S(1)} %get-tuple-element.64) | copy-start | bytes 18436
  17.1 16.8 %copy-start.22 = (f32[1536]{0:T(1024)}, f32[1536]{0:T(1024)S(1)}, u32[]{:S(2)}) copy-start(f32[1536]{0:T(1024)S(1)} %get-tuple-element.65) | copy-start | bytes 18436
  17.2 16.8 %copy-start.23 = (f32[1536]{0:T(1024)}, f32[1536]{0:T(1024)S(1)}, u32[]{:S(2)}) copy-start(f32[1536]{0:T(1024)S(1)} %get-tuple-element.66) | copy-start | bytes 18436
  17.2 16.8 %copy-start.24 = (f32[1536]{0:T(1024)}, f32[1536]{0:T(1024)S(1)}, u32[]{:S(2)}) copy-start(f32[1536]{0:T(1024)S(1)} %get-tuple-element.67) | copy-start | bytes 18436
  17.2 16.8 %copy-start.25 = (f32[1536]{0:T(1024)}, f32[1536]{0:T(1024)S(1)}, u32[]{:S(2)}) copy-start(f32[1536]{0:T(1024)S(1)} %get-tuple-element.68) | copy-start | bytes 18436
  17.2 16.8 %copy-start.26 = (f32[1536]{0:T(1024)}, f32[1536]{0:T(1024)S(1)}, u32[]{:S(2)}) copy-start(f32[1536]{0:T(1024)S(1)} %get-tuple-element.69) | copy-start | bytes 18436
  17.2 16.8 %copy-start.27 = (f32[1536]{0:T(1024)}, f32[1536]{0:T(1024)S(1)}, u32[]{:S(2)}) copy-start(f32[1536]{0:T(1024)S(1)} %get-tuple-element.70) | copy-start | bytes 18436
  17.2 16.8 %copy-start.28 = (f32[1536]{0:T(1024)}, f32[1536]{0:T(1024)S(1)}, u32[]{:S(2)}) copy-start(f32[1536]{0:T(1024)S(1)} %get-tuple-element.71) | copy-start | bytes 18436
  17.2 16.8 %copy-start.29 = (f32[1536]{0:T(1024)}, f32[1536]{0:T(1024)S(1)}, u32[]{:S(2)}) copy-start(f32[1536]{0:T(1024)S(1)} %get-tuple-element.72) | copy-start | bytes 18436
  17.2 16.8 %copy-start.30 = (f32[1536]{0:T(1024)}, f32[1536]{0:T(1024)S(1)}, u32[]{:S(2)}) copy-start(f32[1536]{0:T(1024)S(1)} %get-tuple-element.73) | copy-start | bytes 18436
  17.2 16.8 %copy-start.31 = (f32[1536]{0:T(1024)}, f32[1536]{0:T(1024)S(1)}, u32[]{:S(2)}) copy-start(f32[1536]{0:T(1024)S(1)} %get-tuple-element.74) | copy-start | bytes 18436
  18.2 15.9 %copy-start.37 = (f32[1536]{0:T(1024)}, f32[1536]{0:T(1024)S(1)}, u32[]{:S(2)}) copy-start(f32[1536]{0:T(1024)S(1)} %get-tuple-element.80) | copy-start | bytes 18436
  18.2 15.9 %copy-start.38 = (f32[1536]{0:T(1024)}, f32[1536]{0:T(1024)S(1)}, u32[]{:S(2)}) copy-start(f32[1536]{0:T(1024)S(1)} %get-tuple-element.81) | copy-start | bytes 18436
  18.2 15.9 %copy-start.39 = (f32[1536]{0:T(1024)}, f32[1536]{0:T(1024)S(1)}, u32[]{:S(2)}) copy-start(f32[1536]{0:T(1024)S(1)} %get-tuple-element.82) | copy-start | bytes 18436
  18.2 15.9 %copy-start.40 = (f32[1536]{0:T(1024)}, f32[1536]{0:T(1024)S(1)}, u32[]{:S(2)}) copy-start(f32[1536]{0:T(1024)S(1)} %get-tuple-element.83) | copy-start | bytes 18436
  18.2 15.9 %copy-start.41 = (f32[1536]{0:T(1024)}, f32[1536]{0:T(1024)S(1)}, u32[]{:S(2)}) copy-start(f32[1536]{0:T(1024)S(1)} %get-tuple-element.84) | copy-start | bytes 18436
  18.2 15.9 %copy-start.42 = (f32[1536]{0:T(1024)}, f32[1536]{0:T(1024)S(1)}, u32[]{:S(2)}) copy-start(f32[1536]{0:T(1024)S(1)} %get-tuple-element.85) | copy-start | bytes 18436
  18.2 15.9 %copy-start.43 = (f32[1536]{0:T(1024)}, f32[1536]{0:T(1024)S(1)}, u32[]{:S(2)}) copy-start(f32[1536]{0:T(1024)S(1)} %get-tuple-element.86) | copy-start | bytes 18436
  18.2 15.9 %copy-start.44 = (f32[1536]{0:T(1024)}, f32[1536]{0:T(1024)S(1)}, u32[]{:S(2)}) copy-start(f32[1536]{0:T(1024)S(1)} %get-tuple-element.87) | copy-start | bytes 18436
  18.3 15.9 %copy-start.45 = (f32[1536]{0:T(1024)}, f32[1536]{0:T(1024)S(1)}, u32[]{:S(2)}) copy-start(f32[1536]{0:T(1024)S(1)} %get-tuple-element.88) | copy-start | bytes 18436
  18.3 15.9 %copy-start.46 = (f32[1536]{0:T(1024)}, f32[1536]{0:T(1024)S(1)}, u32[]{:S(2)}) copy-start(f32[1536]{0:T(1024)S(1)} %get-tuple-element.89) | copy-start | bytes 18436
  21.4 6.7 %collective-permute-start.2 = (bf16[1,14,3,1536]{3,2,1,0:T(4,128)(2,1)S(1)}, bf16[1,14,3,1536]{3,2,1,0:T(4,128)(2,1)S(1)}, u32[]{:S(2)}, u32[]{:S(2)}) collective-permute-start(bf16[1,14,3,1536]{3,2,1,0:T(4,128)(2,1)S(1)} %get-tuple-element.115), channel_id=1, source_target_pairs={{0,32},{1,33},{2,34},{3,35},{4,36},{5,37},{6,38},{7,39},{8,40},{9,... | collective-permute-start | bytes 387080 | tf_op jit(solution)/shard_map/ppermute | solution.py:17
  25.8 7.7 %collective-permute-start.3 = (bf16[1,14,3,1536]{3,2,1,0:T(4,128)(2,1)S(1)}, bf16[1,14,3,1536]{3,2,1,0:T(4,128)(2,1)S(1)}, u32[]{:S(2)}, u32[]{:S(2)}) collective-permute-start(bf16[1,14,3,1536]{3,2,1,0:T(4,128)(2,1)S(1)} %get-tuple-element.116), channel_id=1, source_target_pairs={{32,0},{33,1},{34,2},{35,3},{36,4},{37,5},{38,6},{39,7},{40,8},{41... | collective-permute-start | bytes 387080 | tf_op jit(solution)/shard_map/ppermute | solution.py:18
  43.7 73.9 %copy-start.50 = (f32[3072]{0:T(1024)S(1)}, f32[3072]{0:T(1024)}, u32[]{:S(2)}) copy-start(f32[3072]{0:T(1024)} %param.19) | copy-start | bytes 36868
  117.5 103.2 %copy-start.51 = (f32[1536]{0:T(1024)S(1)}, f32[1536]{0:T(1024)}, u32[]{:S(2)}) copy-start(f32[1536]{0:T(1024)} %param.22) | copy-start | bytes 18436
  117.5 103.2 %copy-start.54 = (f32[1536]{0:T(1024)S(1)}, f32[1536]{0:T(1024)}, u32[]{:S(2)}) copy-start(f32[1536]{0:T(1024)} %param.21) | copy-start | bytes 18436
  253.1 6.7 %collective-permute-start.4 = (bf16[1,3,16,1536]{3,2,1,0:T(8,128)(2,1)S(1)}, bf16[1,3,16,1536]{3,2,1,0:T(8,128)(2,1)S(1)}, u32[]{:S(2)}, u32[]{:S(2)}) collective-permute-start(bf16[1,3,16,1536]{3,2,1,0:T(8,128)(2,1)S(1)} %get-tuple-element.119), channel_id=1, source_target_pairs={{0,64},{64,128},{128,192},{1,65},{65,129},{129,193},{2,66},{66,130... | collective-permute-start | bytes 442376 | tf_op jit(solution)/shard_map/ppermute | solution.py:17
  257.2 6.5 %collective-permute-start.5 = (bf16[1,3,16,1536]{3,2,1,0:T(8,128)(2,1)S(1)}, bf16[1,3,16,1536]{3,2,1,0:T(8,128)(2,1)S(1)}, u32[]{:S(2)}, u32[]{:S(2)}) collective-permute-start(bf16[1,3,16,1536]{3,2,1,0:T(8,128)(2,1)S(1)} %get-tuple-element.120), channel_id=1, source_target_pairs={{64,0},{128,64},{192,128},{65,1},{129,65},{193,129},{66,2},{130,66... | collective-permute-start | bytes 442376 | tf_op jit(solution)/shard_map/ppermute | solution.py:18
  263.9 82.3 %collective-permute-start.6 = (bf16[1,14,3,1536]{3,2,1,0:T(4,128)(2,1)S(1)}, bf16[1,14,3,1536]{3,2,1,0:T(4,128)(2,1)S(1)}, u32[]{:S(2)}, u32[]{:S(2)}) collective-permute-start(bf16[1,14,3,1536]{3,2,1,0:T(4,128)(2,1)S(1)} %get-tuple-element.111), channel_id=1, source_target_pairs={{0,32},{1,33},{2,34},{3,35},{4,36},{5,37},{6,38},{7,39},{8,40},{9,... | collective-permute-start | bytes 387080 | tf_op jit(solution)/shard_map/ppermute | solution.py:17
  268.3 78.0 %collective-permute-start.7 = (bf16[1,14,3,1536]{3,2,1,0:T(4,128)(2,1)S(1)}, bf16[1,14,3,1536]{3,2,1,0:T(4,128)(2,1)S(1)}, u32[]{:S(2)}, u32[]{:S(2)}) collective-permute-start(bf16[1,14,3,1536]{3,2,1,0:T(4,128)(2,1)S(1)} %get-tuple-element.112), channel_id=1, source_target_pairs={{32,0},{33,1},{34,2},{35,3},{36,4},{37,5},{38,6},{39,7},{40,8},{41... | collective-permute-start | bytes 387080 | tf_op jit(solution)/shard_map/ppermute | solution.py:18
  270.3 78.0 %copy-start.3 = (bf16[1,8,16,1536]{3,2,1,0:T(8,128)(2,1)S(1)}, bf16[1,8,16,1536]{3,2,1,0:T(8,128)(2,1)}, u32[]{:S(2)}) copy-start(bf16[1,8,16,1536]{3,2,1,0:T(8,128)(2,1)} %param.23) | copy-start | bytes 1179652
  270.3 78.0 %copy-start.10 = (f32[1536]{0:T(1024)S(1)}, f32[1536]{0:T(1024)}, u32[]{:S(2)}) copy-start(f32[1536]{0:T(1024)} %copy-done.9) | copy-start | bytes 18436
  270.3 78.0 %copy-start.12 = (f32[1536]{0:T(1024)S(1)}, f32[1536]{0:T(1024)}, u32[]{:S(2)}) copy-start(f32[1536]{0:T(1024)} %copy-done.11) | copy-start | bytes 18436
  270.4 78.0 %copy-start.14 = (f32[1536]{0:T(1024)S(1)}, f32[1536]{0:T(1024)}, u32[]{:S(2)}) copy-start(f32[1536]{0:T(1024)} %copy-done.13) | copy-start | bytes 18436
  270.4 78.0 %copy-start.16 = (f32[1536]{0:T(1024)S(1)}, f32[1536]{0:T(1024)}, u32[]{:S(2)}) copy-start(f32[1536]{0:T(1024)} %copy-done.15) | copy-start | bytes 18436
  270.4 78.0 %copy-start.18 = (f32[1536]{0:T(1024)S(1)}, f32[1536]{0:T(1024)}, u32[]{:S(2)}) copy-start(f32[1536]{0:T(1024)} %copy-done.17) | copy-start | bytes 18436
  270.4 78.0 %copy-start.20 = (f32[1536]{0:T(1024)S(1)}, f32[1536]{0:T(1024)}, u32[]{:S(2)}) copy-start(f32[1536]{0:T(1024)} %copy-done.19) | copy-start | bytes 18436
  (18 other events, 159.1 us)
Sparse Core Ops, SparseCore 0:
  10.6 106.9 all-gather.2
  120.1 100.5 all-gather.4
  270.4 243.4 all-reduce.2
where the time goes:
time: 523 us; the launch traced here: 522 us
  waiting for transfers between devices  340 us (65%)
  blocking collectives  75.8 us (14%)
  other arithmetic  31.2 us (6%)
  matrix products  28.6 us (5%)
  starting transfers between devices  23.8 us (5%)
  between operations  15.1 us (3%)
  local copies, waits for them, and re-layouts  7.13 us (1%)
    psum x1, waiting for transfers between devices, on_device(): lax.psum((kernel_term, gain_term, scale_term), ('sx', 'sy', 'fsdp'))  158 us
    all_gather x1, waiting for transfers between devices, on_device(): lax.all_gather(w_down, 'fsdp', axis=1, tiled=True)  96.8 us
    psum x1, blocking collectives, on_device(): lax.psum((kernel_term, gain_term, scale_term), ('sx', 'sy', 'fsdp'))  75.8 us
    all_gather x1, waiting for transfers between devices, on_device(): lax.all_gather(w_up, 'fsdp', axis=0, tiled=True)  71.9 us
    ppermute x4, starting transfers between devices, with_halo(): before = lax.ppermute(last, axis, up)  17.3 us
    dot_general x1, matrix products, on_device(): lax.dot_general(d_pre, up_full, (((1,), (1,)), ((), ())), preferred_eleme...  13.3 us
    ppermute x4, waiting for transfers between devices, with_halo(): after = lax.ppermute(initial, axis, down)  12.2 us
  transfers between devices with their start and end apart: 11, of which 7 were waited for; matrix products, arithmetic and copies ran while one was open for 6% of the time, Pallas kernels for 0%

commit v1 on v0

--- a/solution.py
+++ b/solution.py
@@ -5,6 +5,12 @@
 
 CG = 128
 KW = 7
+
+
+def _raise_runs(sample):
+    return jnp.concatenate(
+        lax.all_to_all(jnp.stack([sample] * lax.axis_size("fsdp"), 0), "fsdp", 0, 0), 1
+    )
 
 
 def with_halo(shard, sides, width):
@@ -43,10 +49,7 @@
     factor = jnp.exp2(x_exp[0].astype(jnp.float32))
     grouped = code.astype(jnp.float32).reshape(rows, cols, chans // CG, CG) * factor[..., None]
     scaled = grouped.reshape(rows, cols, chans).astype(jnp.bfloat16)
-    up_full, down_full = (
-        lax.all_gather(w_up, "fsdp", axis=0, tiled=True),
-        lax.all_gather(w_down, "fsdp", axis=1, tiled=True),
-    )
+    up_full, down_full = (lax.all_gather(w_up, "fsdp", axis=0, tiled=True), _raise_runs(w_down))
     padded_x = with_halo(scaled[None], (("sx", 1), ("sy", 2)), 3)[0].astype(jnp.float32)
     conv = jnp.zeros((rows, cols, chans), jnp.float32) + dw_bias
     for i in range(KW):

time: 523 us -> 597 us (1.14)
  waiting for transfers between devices: 340 us -> 386 us
  starting transfers between devices: 23.8 us -> 46.4 us
  local copies, waits for them, and re-layouts: 7.13 us -> 13.5 us
    all_gather x1, waiting for transfers between devices: 71.9 us -> 211 us  [on_device(): lax.all_gather(w_up, 'fsdp', axis=0, tiled=True)]
    all_gather x1 -> x0, waiting for transfers between devices: 96.8 us -> none  [on_device(): lax.all_gather(w_down, 'fsdp', axis=1, tiled=True)]
    all_to_all x0 -> x1, starting transfers between devices: none -> 12.3 us  [_raise_runs(): lax.all_to_all(jnp.stack([sample] * lax.axis_size('fsdp'), 0), 'fsdp', 0, 0)]
    ppermute x4, waiting for transfers between devices: 12.2 us -> 1.62 us  [with_halo(): after = lax.ppermute(initial, axis, down)]
    all_to_all x0 -> x1, waiting for transfers between devices: none -> 8.99 us  [_raise_runs(): lax.all_to_all(jnp.stack([sample] * lax.axis_size('fsdp'), 0), 'fsdp', 0, 0)]
    ppermute x4, starting transfers between devices: 17.3 us -> 24.7 us  [with_halo(): before = lax.ppermute(last, axis, up)]
where the time goes in v1:
time: 597 us
  waiting for transfers between devices  386 us (65%)
  blocking collectives  75 us (13%)
  starting transfers between devices  46.4 us (8%)
  other arithmetic  31.4 us (5%)
  matrix products  27.9 us (5%)
  between operations  16.1 us (3%)
  local copies, waits for them, and re-layouts  13.5 us (2%)
    all_gather x1, waiting for transfers between devices, on_device(): lax.all_gather(w_up, 'fsdp', axis=0, tiled=True)  211 us
    psum x1, waiting for transfers between devices, on_device(): lax.psum((kernel_term, gain_term, scale_term), ('sx', 'sy', 'fsdp'))  161 us
    psum x1, blocking collectives, on_device(): lax.psum((kernel_term, gain_term, scale_term), ('sx', 'sy', 'fsdp'))  75 us
    ppermute x4, starting transfers between devices, with_halo(): before = lax.ppermute(last, axis, up)  24.7 us
    dot_general x1, matrix products, on_device(): lax.dot_general(d_pre, up_full, (((1,), (1,)), ((), ())), preferred_eleme...  13.4 us
    all_to_all x1, starting transfers between devices, _raise_runs(): lax.all_to_all(jnp.stack([sample] * lax.axis_size('fsdp'), 0), 'fsdp', 0, 0)  12.3 us
  transfers between devices with their start and end apart: 11, of which 7 were waited for; matrix products, arithmetic and copies ran while one was open for 6% of the time, Pallas kernels for 0%

profile of v1, /device:TPU:1, one launch (start us, length us, event | category | flops | bytes accessed | tf_op | source)
XLA Modules:
  0.0 596.7 jit_solution(5169429415238454625)
XLA Ops:
  7.2 0.7 all-gather.2.cloned.1.call-update
  7.9 5.9 stack.227
  13.8 12.3 %all-to-all-start = ((bf16[32,3072,48]{1,2,0:T(8,128)(2,1)}), bf16[32,3072,48]{1,2,0:T(8,128)(2,1)}, u32[]{:S(2)}, u32[]{:S(2)}) async-start(bf16[32,3072,48]{1,2,0:T(8,128)(2,1)} %stack.227), calls=%async_computation | async-start | bytes 18874368 | tf_op jit(solution)/shard_map/all_to_all | solution.py:12
  26.2 0.1 copy.19
  26.3 0.3 mul.1065
  26.6 0.1 mul.1066
  26.8 0.3 copy-done.3
  27.2 2.9 collective-permute-start.1
  30.1 3.0 collective-permute-start
  33.1 0.3 slice_reduce_fusion.48
  33.5 0.9 slice_reduce_fusion.47
  34.6 0.6 collective-permute-done
  35.2 0.1 pad_maximum_fusion.3
  35.3 1.3 collective-permute-start.3
  36.6 5.5 collective-permute-start.2
  42.1 0.8 slice_reduce_fusion.46
  42.9 1.6 collective-permute-done.3
  44.5 1.4 collective-permute-done.2
  45.9 0.4 fusion.7
  46.6 9.4 %fusion.83 = (f32[8,16]{1,0:T(8,128)S(1)}, f32[8,16,1536]{2,1,0:T(8,128)S(1)}) fusion(f32[14,22,1536]{2,1,0:T(8,128)S(1)} %fusion.7, f32[1536]{0:T(1024)} %get-tuple-element.103, f32[1536]{0:T(1024)} %get-tuple-element.104, f32[1536]{0:T(1024)S(1)} %get-tuple-element.57, f32[1536]{0:T(1024)S(1)} %get-tuple-element.58, f32[1536]{0:T(1024)S(1)} %get-tuple-element.59, ...), kind=kLoop, calls=%fused_computation.265 | loop fusion | flops 19464064 | bytes 39629312 | tf_op jit(solution)/shard_map/reduce_sum | solution.py:58
  56.0 0.2 multiply_reduce_fusion.52
  56.3 1.7 add_convert_fusion.1
  57.9 211.2 %all-gather.2.cloned.1.call-done = bf16[1536,3072]{1,0:T(8,128)(2,1)} async-done(((bf16[48,3072]{1,0:T(8,128)(2,1)}), bf16[1536,3072]{1,0:T(8,128)(2,1)}) %all-gather.2.cloned.1.call-update) | async-done | bytes 9437200 | tf_op jit(solution)/shard_map/all_gather | solution.py:52
  269.2 6.4 %convolution_add_fusion = f32[128,3072]{1,0:T(8,128)} fusion(bf16[128,1536]{1,0:T(8,128)(2,1)} %bitcast.54, bf16[1536,3072]{1,0:T(8,128)(2,1)} %all-gather.2.cloned.1.call-done, f32[3072]{0:T(1024)S(1)} %copy-done.94), kind=kOutput, calls=%fused_computation | convolution fusion | flops 1208352768 | bytes 11415552 | tf_op jit(solution)/shard_map/dot_general | solution.py:63
  275.6 9.0 %all-to-all-done = bf16[32,3072,48]{1,2,0:T(8,128)(2,1)} async-done(((bf16[32,3072,48]{1,2,0:T(8,128)(2,1)}), bf16[32,3072,48]{1,2,0:T(8,128)(2,1)}, u32[]{:S(2)}, u32[]{:S(2)}) %all-to-all-start) | async-done | bytes 9437216 | tf_op jit(solution)/shard_map/all_to_all | solution.py:12
  284.6 8.1 %fusion.60 = (f32[1536]{0:T(1024)}, f32[128,1536]{1,0:T(8,128)S(1)}) fusion(bf16[1,8,16,1536]{3,2,1,0:T(8,128)(2,1)} %param.23, f32[1536]{0:T(1024)S(1)} %copy-done.96, bf16[3072,1536]{0,1:T(8,128)(2,1)} %bitcast.5, f32[128,3072]{1,0:T(8,128)} %convolution_add_fusion), kind=kOutput, calls=%fused_computation.116 | convolution fusion | flops 1212283392 | bytes 12201984 | tf_op jit(solution)/shard_map/dot_general | solution.py:65
  292.7 1.1 multiply_convert_fusion.2
  293.8 13.4 %multiply_reduce_fusion.51 = (f32[128]{0:T(128)S(1)}, f32[128,1536]{1,0:T(8,128)}) fusion(f32[1536]{0:T(1024)S(1)} %copy-done.7, bf16[1536,3072]{1,0:T(8,128)(2,1)} %all-gather.2.cloned.1.call-done, f32[128,3072]{1,0:T(8,128)} %convolution_add_fusion, bf16[128,1536]{1,0:T(8,128)(2,1)} %bitcast.56, bf16[3072,1536]{0,1:T(8,128)(2,1)} %bitcast.5), kind=kOutput, calls=%fused_computation.169 | convolution fusion | flops 2424176640 | bytes 21633536 | tf_op jit(solution)/shard_map/dot_general | solution.py:75
  307.1 2.3 multiply_reduce_fusion
  309.5 0.1 div.17
  309.5 4.3 multiply_reduce_fusion.1
  313.8 1.9 multiply_reduce_fusion.19
  315.9 1.4 multiply_reduce_fusion.37
  317.4 3.9 collective-permute-start.5
  321.3 10.7 %collective-permute-start.4 = (bf16[1,3,16,1536]{3,2,1,0:T(8,128)(2,1)S(1)}, bf16[1,3,16,1536]{3,2,1,0:T(8,128)(2,1)S(1)}, u32[]{:S(2)}, u32[]{:S(2)}) collective-permute-start(bf16[1,3,16,1536]{3,2,1,0:T(8,128)(2,1)S(1)} %get-tuple-element.117), channel_id=1, source_target_pairs={{0,64},{64,128},{128,192},{1,65},{65,129},{129,193},{2,66},{66,130... | collective-permute-start | bytes 442376 | tf_op jit(solution)/shard_map/ppermute | solution.py:23
  332.9 0.1 stack.253
  333.5 1.0 collective-permute-done.4
  334.5 0.1 fusion.82
  334.6 0.1 fusion.84
  334.8 1.3 collective-permute-start.7
  336.1 5.5 collective-permute-start.6
  341.6 0.7 copy-done.2
  342.8 75.0 %all-reduce = (f32[1536]{0:T(1024)}, f32[1536]{0:T(1024)}) all-reduce(f32[1536]{0:T(1024)} %get-tuple-element.54, f32[1536]{0:T(1024)} %get-tuple-element.125), channel_id=1, replica_groups=mesh['sx'=4,'sy'=2,'fsdp'=32] {'sx','sy','fsdp'}, use_global_device_ids=true, to_apply=%region_55.0 | all-reduce | flops 3072 | bytes 24576 | tf_op jit(solution)/shard_map/psum | solution.py:104
  417.8 0.7 copy-done.5
  418.5 1.4 maximum_convert_fusion
  420.3 6.9 %fusion.71 = bf16[1,8,16,1536]{3,2,1,0:T(8,128)(2,1)} fusion(f32[14,22,1536]{2,1,0:T(8,128)S(1)} %maximum_convert_fusion, f32[1536]{0:T(1024)} %get-tuple-element.103, f32[1536]{0:T(1024)} %get-tuple-element.104, f32[1536]{0:T(1024)S(1)} %get-tuple-element.57, f32[1536]{0:T(1024)S(1)} %get-tuple-element.58, f32[1536]{0:T(1024)S(1)} %get-tuple-element.59, ...), kind=kLoop, calls=%fused_computation.189 | loop fusion | flops 19660800 | bytes 39622656 | tf_op jit(solution)/shard_map/broadcast_in_dim | solution.py:107
  427.2 160.9 %all-reduce.3.cloned.1.call-done = f32[7,7,1536]{2,1,0:T(8,128)} async-done(((f32[7,7,1536]{2,1,0:T(8,128)}), f32[7,7,1536]{2,1,0:T(8,128)}) %all-reduce.3.cloned.1.call-update) | async-done | bytes 301072 | tf_op jit(solution)/shard_map/psum | solution.py:104
  588.1 1.7 copy.27
  (268 shorter events, 1.5 us)
Async XLA Ops:
  7.2 262.0 %all-gather.2.cloned.1.call-start = ((), (), s32[]{:S(2)}) async-start(), calls=%async_computation.1 | async-start | bytes 9732096 | tf_op jit(solution)/shard_map/all_gather | solution.py:52
  13.8 270.8 %all-to-all-start = ((bf16[32,3072,48]{1,2,0:T(8,128)(2,1)}), bf16[32,3072,48]{1,2,0:T(8,128)(2,1)}, u32[]{:S(2)}, u32[]{:S(2)}) async-start(bf16[32,3072,48]{1,2,0:T(8,128)(2,1)} %stack.227), calls=%async_computation | async-start | bytes 18874368 | tf_op jit(solution)/shard_map/all_to_all | solution.py:12
  26.1 562.0 %all-reduce.3.cloned.1.call-start = ((), (), s32[]{:S(2)}) async-start(), calls=%async_computation.2 | async-start | bytes 688128 | tf_op jit(solution)/shard_map/psum | solution.py:104
  27.2 7.4 %collective-permute-start.1 = (bf16[1,3,16,1536]{3,2,1,0:T(8,128)(2,1)S(1)}, bf16[1,3,16,1536]{3,2,1,0:T(8,128)(2,1)S(1)}, u32[]{:S(2)}, u32[]{:S(2)}) collective-permute-start(bf16[1,3,16,1536]{3,2,1,0:T(8,128)(2,1)S(1)} %get-tuple-element.120), channel_id=1, source_target_pairs={{64,0},{128,64},{192,128},{65,1},{129,65},{193,129},{66,2},{130,66... | collective-permute-start | bytes 442376 | tf_op jit(solution)/shard_map/ppermute | solution.py:24
  30.1 5.1 collective-permute-start
  35.3 9.2 %collective-permute-start.3 = (bf16[1,14,3,1536]{3,2,1,0:T(4,128)(2,1)S(1)}, bf16[1,14,3,1536]{3,2,1,0:T(4,128)(2,1)S(1)}, u32[]{:S(2)}, u32[]{:S(2)}) collective-permute-start(bf16[1,14,3,1536]{3,2,1,0:T(4,128)(2,1)S(1)} %get-tuple-element.116), channel_id=1, source_target_pairs={{32,0},{33,1},{34,2},{35,3},{36,4},{37,5},{38,6},{39,7},{40,8},{41... | collective-permute-start | bytes 387080 | tf_op jit(solution)/shard_map/ppermute | solution.py:24
  36.6 9.3 %collective-permute-start.2 = (bf16[1,14,3,1536]{3,2,1,0:T(4,128)(2,1)S(1)}, bf16[1,14,3,1536]{3,2,1,0:T(4,128)(2,1)S(1)}, u32[]{:S(2)}, u32[]{:S(2)}) collective-permute-start(bf16[1,14,3,1536]{3,2,1,0:T(4,128)(2,1)S(1)} %get-tuple-element.115), channel_id=1, source_target_pairs={{0,32},{1,33},{2,34},{3,35},{4,36},{5,37},{6,38},{7,39},{8,40},{9,... | collective-permute-start | bytes 387080 | tf_op jit(solution)/shard_map/ppermute | solution.py:23
  56.0 213.2 %copy-start.94 = (f32[3072]{0:T(1024)S(1)}, f32[3072]{0:T(1024)}, u32[]{:S(2)}) copy-start(f32[3072]{0:T(1024)} %param.19) | copy-start | bytes 36868
  317.4 16.1 %collective-permute-start.5 = (bf16[1,3,16,1536]{3,2,1,0:T(8,128)(2,1)S(1)}, bf16[1,3,16,1536]{3,2,1,0:T(8,128)(2,1)S(1)}, u32[]{:S(2)}, u32[]{:S(2)}) collective-permute-start(bf16[1,3,16,1536]{3,2,1,0:T(8,128)(2,1)S(1)} %get-tuple-element.118), channel_id=1, source_target_pairs={{64,0},{128,64},{192,128},{65,1},{129,65},{193,129},{66,2},{130,66... | collective-permute-start | bytes 442376 | tf_op jit(solution)/shard_map/ppermute | solution.py:24
  321.3 13.2 %collective-permute-start.4 = (bf16[1,3,16,1536]{3,2,1,0:T(8,128)(2,1)S(1)}, bf16[1,3,16,1536]{3,2,1,0:T(8,128)(2,1)S(1)}, u32[]{:S(2)}, u32[]{:S(2)}) collective-permute-start(bf16[1,3,16,1536]{3,2,1,0:T(8,128)(2,1)S(1)} %get-tuple-element.117), channel_id=1, source_target_pairs={{0,64},{64,128},{128,192},{1,65},{65,129},{129,193},{2,66},{66,130... | collective-permute-start | bytes 442376 | tf_op jit(solution)/shard_map/ppermute | solution.py:23
  334.8 83.0 %collective-permute-start.7 = (bf16[1,14,3,1536]{3,2,1,0:T(4,128)(2,1)S(1)}, bf16[1,14,3,1536]{3,2,1,0:T(4,128)(2,1)S(1)}, u32[]{:S(2)}, u32[]{:S(2)}) collective-permute-start(bf16[1,14,3,1536]{3,2,1,0:T(4,128)(2,1)S(1)} %get-tuple-element.112), channel_id=1, source_target_pairs={{32,0},{33,1},{34,2},{35,3},{36,4},{37,5},{38,6},{39,7},{40,8},{41... | collective-permute-start | bytes 387080 | tf_op jit(solution)/shard_map/ppermute | solution.py:24
  336.1 81.7 %collective-permute-start.6 = (bf16[1,14,3,1536]{3,2,1,0:T(4,128)(2,1)S(1)}, bf16[1,14,3,1536]{3,2,1,0:T(4,128)(2,1)S(1)}, u32[]{:S(2)}, u32[]{:S(2)}) collective-permute-start(bf16[1,14,3,1536]{3,2,1,0:T(4,128)(2,1)S(1)} %get-tuple-element.111), channel_id=1, source_target_pairs={{0,32},{1,33},{2,34},{3,35},{4,36},{5,37},{6,38},{7,39},{8,40},{9,... | collective-permute-start | bytes 387080 | tf_op jit(solution)/shard_map/ppermute | solution.py:23
  342.4 77.5 %copy-start.1 = (bf16[1,8,16,1536]{3,2,1,0:T(8,128)(2,1)S(1)}, bf16[1,8,16,1536]{3,2,1,0:T(8,128)(2,1)}, u32[]{:S(2)}) copy-start(bf16[1,8,16,1536]{3,2,1,0:T(8,128)(2,1)} %param.23) | copy-start | bytes 1179652
  342.4 77.5 %copy-start.9 = (f32[1536]{0:T(1024)S(1)}, f32[1536]{0:T(1024)}, u32[]{:S(2)}) copy-start(f32[1536]{0:T(1024)} %copy-done.8) | copy-start | bytes 18436
  342.4 77.5 %copy-start.11 = (f32[1536]{0:T(1024)S(1)}, f32[1536]{0:T(1024)}, u32[]{:S(2)}) copy-start(f32[1536]{0:T(1024)} %copy-done.10) | copy-start | bytes 18436
  342.4 77.5 %copy-start.13 = (f32[1536]{0:T(1024)S(1)}, f32[1536]{0:T(1024)}, u32[]{:S(2)}) copy-start(f32[1536]{0:T(1024)} %copy-done.12) | copy-start | bytes 18436
  342.4 77.5 %copy-start.15 = (f32[1536]{0:T(1024)S(1)}, f32[1536]{0:T(1024)}, u32[]{:S(2)}) copy-start(f32[1536]{0:T(1024)} %copy-done.14) | copy-start | bytes 18436
  342.4 77.5 %copy-start.17 = (f32[1536]{0:T(1024)S(1)}, f32[1536]{0:T(1024)}, u32[]{:S(2)}) copy-start(f32[1536]{0:T(1024)} %copy-done.16) | copy-start | bytes 18436
  342.4 77.5 %copy-start.19 = (f32[1536]{0:T(1024)S(1)}, f32[1536]{0:T(1024)}, u32[]{:S(2)}) copy-start(f32[1536]{0:T(1024)} %copy-done.18) | copy-start | bytes 18436
  342.4 77.5 %copy-start.21 = (f32[1536]{0:T(1024)S(1)}, f32[1536]{0:T(1024)}, u32[]{:S(2)}) copy-start(f32[1536]{0:T(1024)} %copy-done.20) | copy-start | bytes 18436
  342.5 77.5 %copy-start.23 = (f32[1536]{0:T(1024)S(1)}, f32[1536]{0:T(1024)}, u32[]{:S(2)}) copy-start(f32[1536]{0:T(1024)} %copy-done.22) | copy-start | bytes 18436
  342.5 77.5 %copy-start.25 = (f32[1536]{0:T(1024)S(1)}, f32[1536]{0:T(1024)}, u32[]{:S(2)}) copy-start(f32[1536]{0:T(1024)} %copy-done.24) | copy-start | bytes 18436
  342.5 77.5 %copy-start.27 = (f32[1536]{0:T(1024)S(1)}, f32[1536]{0:T(1024)}, u32[]{:S(2)}) copy-start(f32[1536]{0:T(1024)} %copy-done.26) | copy-start | bytes 18436
  342.5 77.5 %copy-start.29 = (f32[1536]{0:T(1024)S(1)}, f32[1536]{0:T(1024)}, u32[]{:S(2)}) copy-start(f32[1536]{0:T(1024)} %copy-done.28) | copy-start | bytes 18436
  342.5 77.5 %copy-start.31 = (f32[1536]{0:T(1024)S(1)}, f32[1536]{0:T(1024)}, u32[]{:S(2)}) copy-start(f32[1536]{0:T(1024)} %copy-done.30) | copy-start | bytes 18436
  342.5 77.5 %copy-start.33 = (f32[1536]{0:T(1024)S(1)}, f32[1536]{0:T(1024)}, u32[]{:S(2)}) copy-start(f32[1536]{0:T(1024)} %copy-done.32) | copy-start | bytes 18436
  342.5 77.5 %copy-start.35 = (f32[1536]{0:T(1024)S(1)}, f32[1536]{0:T(1024)}, u32[]{:S(2)}) copy-start(f32[1536]{0:T(1024)} %copy-done.34) | copy-start | bytes 18436
  342.5 77.5 %copy-start.37 = (f32[1536]{0:T(1024)S(1)}, f32[1536]{0:T(1024)}, u32[]{:S(2)}) copy-start(f32[1536]{0:T(1024)} %copy-done.36) | copy-start | bytes 18436
  342.5 77.5 %copy-start.39 = (f32[1536]{0:T(1024)S(1)}, f32[1536]{0:T(1024)}, u32[]{:S(2)}) copy-start(f32[1536]{0:T(1024)} %copy-done.38) | copy-start | bytes 18436
  342.5 77.5 %copy-start.41 = (f32[1536]{0:T(1024)S(1)}, f32[1536]{0:T(1024)}, u32[]{:S(2)}) copy-start(f32[1536]{0:T(1024)} %copy-done.40) | copy-start | bytes 18436
  342.6 77.5 %copy-start.43 = (f32[1536]{0:T(1024)S(1)}, f32[1536]{0:T(1024)}, u32[]{:S(2)}) copy-start(f32[1536]{0:T(1024)} %copy-done.42) | copy-start | bytes 18436
  342.6 77.5 %copy-start.45 = (f32[1536]{0:T(1024)S(1)}, f32[1536]{0:T(1024)}, u32[]{:S(2)}) copy-start(f32[1536]{0:T(1024)} %copy-done.44) | copy-start | bytes 18436
  342.6 77.5 %copy-start.47 = (f32[1536]{0:T(1024)S(1)}, f32[1536]{0:T(1024)}, u32[]{:S(2)}) copy-start(f32[1536]{0:T(1024)} %copy-done.46) | copy-start | bytes 18436
  342.6 77.5 %copy-start.49 = (f32[1536]{0:T(1024)S(1)}, f32[1536]{0:T(1024)}, u32[]{:S(2)}) copy-start(f32[1536]{0:T(1024)} %copy-done.48) | copy-start | bytes 18436
  342.6 77.5 %copy-start.51 = (f32[1536]{0:T(1024)S(1)}, f32[1536]{0:T(1024)}, u32[]{:S(2)}) copy-start(f32[1536]{0:T(1024)} %copy-done.50) | copy-start | bytes 18436
  342.6 77.5 %copy-start.53 = (f32[1536]{0:T(1024)S(1)}, f32[1536]{0:T(1024)}, u32[]{:S(2)}) copy-start(f32[1536]{0:T(1024)} %copy-done.52) | copy-start | bytes 18436
  342.6 77.5 %copy-start.55 = (f32[1536]{0:T(1024)S(1)}, f32[1536]{0:T(1024)}, u32[]{:S(2)}) copy-start(f32[1536]{0:T(1024)} %copy-done.54) | copy-start | bytes 18436
  342.6 77.5 %copy-start.57 = (f32[1536]{0:T(1024)S(1)}, f32[1536]{0:T(1024)}, u32[]{:S(2)}) copy-start(f32[1536]{0:T(1024)} %copy-done.56) | copy-start | bytes 18436
  342.6 77.5 %copy-start.59 = (f32[1536]{0:T(1024)S(1)}, f32[1536]{0:T(1024)}, u32[]{:S(2)}) copy-start(f32[1536]{0:T(1024)} %copy-done.58) | copy-start | bytes 18436
  342.6 77.5 %copy-start.61 = (f32[1536]{0:T(1024)S(1)}, f32[1536]{0:T(1024)}, u32[]{:S(2)}) copy-start(f32[1536]{0:T(1024)} %copy-done.60) | copy-start | bytes 18436
  342.7 77.5 %copy-start.63 = (f32[1536]{0:T(1024)S(1)}, f32[1536]{0:T(1024)}, u32[]{:S(2)}) copy-start(f32[1536]{0:T(1024)} %copy-done.62) | copy-start | bytes 18436
  342.7 77.5 %copy-start.64 = (f32[1536]{0:T(1024)S(1)}, f32[1536]{0:T(1024)}, u32[]{:S(2)}) copy-start(f32[1536]{0:T(1024)} %get-tuple-element.92) | copy-start | bytes 18436
  342.7 77.5 %copy-start.65 = (f32[1536]{0:T(1024)S(1)}, f32[1536]{0:T(1024)}, u32[]{:S(2)}) copy-start(f32[1536]{0:T(1024)} %get-tuple-element.93) | copy-start | bytes 18436
  342.7 77.5 %copy-start.66 = (f32[1536]{0:T(1024)S(1)}, f32[1536]{0:T(1024)}, u32[]{:S(2)}) copy-start(f32[1536]{0:T(1024)} %get-tuple-element.94) | copy-start | bytes 18436
  342.7 77.5 %copy-start.67 = (f32[1536]{0:T(1024)S(1)}, f32[1536]{0:T(1024)}, u32[]{:S(2)}) copy-start(f32[1536]{0:T(1024)} %get-tuple-element.95) | copy-start | bytes 18436
  342.7 77.5 %copy-start.68 = (f32[1536]{0:T(1024)S(1)}, f32[1536]{0:T(1024)}, u32[]{:S(2)}) copy-start(f32[1536]{0:T(1024)} %get-tuple-element.96) | copy-start | bytes 18436
  342.7 77.5 %copy-start.69 = (f32[1536]{0:T(1024)S(1)}, f32[1536]{0:T(1024)}, u32[]{:S(2)}) copy-start(f32[1536]{0:T(1024)} %get-tuple-element.97) | copy-start | bytes 18436
  342.7 77.5 %copy-start.70 = (f32[1536]{0:T(1024)S(1)}, f32[1536]{0:T(1024)}, u32[]{:S(2)}) copy-start(f32[1536]{0:T(1024)} %get-tuple-element.98) | copy-start | bytes 18436
  (60 other events, 1015.5 us)
Sparse Core Ops, SparseCore 0:
  10.6 258.5 all-gather.1
  342.5 245.5 all-reduce.2
